TPU v7x, 32 devices: a whole 2x2x4 slice. The times are simulated.
32 devices in a mesh: aa: 4 (over x, core), ba: 4 (over z), col: 2 (over y).
Axes of the slice: x: 2, y: 2, z: 4, core: 2. Of those that a mesh axis runs over, the one named last changes fastest.
Arguments:
- inputs: float32 [64, 128, 32, 128], P('aa', 'ba', 'col'), may hold values from -6 to 6
- cotangent: float32 [64, 128, 32, 128], P('aa', 'ba', 'col'), may hold values from -6 to 6
- w_gate: float32 [128, 128], replicated, may hold values from -0.5 to 0.5
- w_value: float32 [128, 128], replicated, may hold values from -0.5 to 0.5
- mix_first: float32 [64, 64], replicated, may hold values from -0.75 to 0.75
- mix_second: float32 [128, 128], replicated, may hold values from -0.5 to 0.5
- mix_third: float32 [32, 32], replicated, may hold values from -1 to 1
- twiddle_first: float32 [64, 128, 32], P('aa', 'ba', 'col'), may hold values from 0.4 to 1.6
- twiddle_second: float32 [64, 128, 32], P('aa', 'ba', 'col'), may hold values from 0.4 to 1.6
- twiddle_third: float32 [64, 128, 32], P('aa', 'ba', 'col'), may hold values from 0.4 to 1.6
Outputs:
- output: float32 [64, 128, 32, 128], P('aa', 'ba', 'col')
- grad_inputs: float32 [64, 128, 32, 128], P('aa', 'ba', 'col')
- grad_gate: float32 [128, 128], replicated
- grad_value: float32 [128, 128], replicated
- grad_first: float32 [64, 64], replicated
- grad_second: float32 [128, 128], replicated
- grad_third: float32 [32, 32], replicated
All inputs are finite; a program needn't handle non-finite values.
Results may differ from a plain program's by a relative error of at most 0.00016.
Values sent between devices are 32-bit elements; how exact they have to be, the bound alone decides.
A program may use at most 192 MiB of HBM per device.

v0:
```python
import jax
import jax.numpy as jnp
from jax import lax
from jax.sharding import PartitionSpec as P


def on_device(
    inputs,
    cotangent,
    w_gate,
    w_value,
    mix_first,
    mix_second,
    mix_third,
    twiddle_first,
    twiddle_second,
    twiddle_third,
):
    highest = lax.Precision.HIGHEST
    across_first = lax.axis_size("aa")
    across_second = lax.axis_size("ba")
    first_width = mix_first.shape[0]
    second_width = mix_second.shape[0]
    local_second = second_width // across_second
    pair_width = local_second // across_first
    gate = jnp.einsum("ijkc,cd->ijkd", inputs, w_gate, precision=highest)
    value = jnp.einsum("ijkc,cd->ijkd", inputs, w_value, precision=highest)
    sigmoid_gate = jax.nn.sigmoid(gate)
    first_home = twiddle_first[..., None] * value
    home_rows = inputs.shape[0]
    home_cols = inputs.shape[1]
    local_third = inputs.shape[2]
    channels = inputs.shape[3]
    part_rows = first_width // (across_first * across_second)
    first_in, second_scale, third_scale = (
        lax.all_to_all(first_home, "aa", split_axis=1, concat_axis=0, tiled=True),
        lax.all_to_all(twiddle_second, "aa", split_axis=1, concat_axis=0, tiled=True),
        lax.all_to_all(twiddle_third, "aa", split_axis=1, concat_axis=0, tiled=True),
    )
    first_out = jnp.einsum("xi,iqkc->xqkc", mix_first, first_in, precision=highest)
    second_in_first = second_scale[..., None] * first_out
    split_values = second_in_first.reshape(
        across_first, across_second, part_rows, 1, 1, pair_width, local_third, channels
    )
    split_scale = third_scale.reshape(
        across_first, across_second, part_rows, 1, 1, pair_width, local_third
    )
    moved_values, moved_scale = (
        lax.all_to_all(
            lax.all_to_all(split_values, "aa", split_axis=0, concat_axis=4, tiled=True),
            "ba",
            split_axis=1,
            concat_axis=3,
            tiled=True,
        ),
        lax.all_to_all(
            lax.all_to_all(split_scale, "aa", split_axis=0, concat_axis=4, tiled=True),
            "ba",
            split_axis=1,
            concat_axis=3,
            tiled=True,
        ),
    )
    second_in = moved_values.reshape(part_rows, second_width, local_third, channels)
    third_local = moved_scale.reshape(part_rows, second_width, local_third)
    second_out = jnp.einsum("yj,pjkc->pykc", mix_second, second_in, precision=highest)
    third_in = (third_local[..., None] * second_out).reshape(
        1, part_rows, second_width, local_third, channels
    )
    third_gathered = lax.all_to_all(
        lax.all_to_all(third_in, "ba", split_axis=2, concat_axis=0, tiled=True),
        "col",
        split_axis=4,
        concat_axis=3,
        tiled=True,
    )
    mixed_third = jnp.einsum("zk,abjkc->abjzc", mix_third, third_gathered, precision=highest)
    mixed = lax.all_to_all(mixed_third, "col", split_axis=3, concat_axis=4, tiled=True).reshape(
        home_rows, home_cols, local_third, channels
    )
    output = sigmoid_gate * mixed
    grad_mixed = cotangent * sigmoid_gate
    grad_gate_act = cotangent * mixed * sigmoid_gate * (1.0 - sigmoid_gate)
    grad_split = grad_mixed.reshape(across_second, part_rows, home_cols, local_third, channels)
    upstream = lax.all_to_all(grad_split, "col", split_axis=4, concat_axis=3, tiled=True)
    grad_third_in = jnp.einsum("zk,abjzc->abjkc", mix_third, upstream, precision=highest)
    raw_third = jnp.einsum("abjzc,abjkc->zk", upstream, third_gathered, precision=highest)
    grad_third_moved = lax.all_to_all(
        lax.all_to_all(grad_third_in, "ba", split_axis=0, concat_axis=2, tiled=True),
        "col",
        split_axis=3,
        concat_axis=4,
        tiled=True,
    ).reshape(part_rows, second_width, local_third, channels)
    grad_second_out = third_local[..., None] * grad_third_moved
    raw_columns = jnp.einsum("pykc,pjkc->yj", grad_second_out, second_in, precision=highest)
    grad_second_in = jnp.einsum("yj,pykc->pjkc", mix_second, grad_second_out, precision=highest)
    grad_split_second = grad_second_in.reshape(
        1, 1, part_rows, across_second, across_first, pair_width, local_third, channels
    )
    grad_back = lax.all_to_all(
        lax.all_to_all(grad_split_second, "aa", split_axis=4, concat_axis=0, tiled=True),
        "ba",
        split_axis=3,
        concat_axis=1,
        tiled=True,
    )
    grad_first_moved = grad_back.reshape(first_width, pair_width, local_third, channels)
    grad_first_out = second_scale[..., None] * grad_first_moved
    raw_first = jnp.einsum("xqkc,iqkc->xi", grad_first_out, first_in, precision=highest)
    grad_first_in = jnp.einsum("xi,xqkc->iqkc", mix_first, grad_first_out, precision=highest)
    grad_first_home = lax.all_to_all(grad_first_in, "aa", split_axis=0, concat_axis=1, tiled=True)
    grad_value_act = twiddle_first[..., None] * grad_first_home
    grad_inputs = jnp.einsum(
        "ijkd,cd->ijkc", grad_gate_act, w_gate, precision=highest
    ) + jnp.einsum("ijkd,cd->ijkc", grad_value_act, w_value, precision=highest)
    raw_gate = jnp.einsum("ijkc,ijkd->cd", inputs, grad_gate_act, precision=highest)
    raw_value = jnp.einsum("ijkc,ijkd->cd", inputs, grad_value_act, precision=highest)
    summed = lax.psum((raw_gate, raw_value, raw_first, raw_columns, raw_third), ("aa", "ba", "col"))
    factor = float(mix_first.shape[0] * mix_second.shape[0] * mix_third.shape[0]) ** (-0.5)
    return (
        output,
        grad_inputs,
        summed[0] * factor,
        summed[1] * factor,
        summed[2] * factor,
        summed[3] * factor,
        summed[4] * factor,
    )


def solution(mesh):
    return jax.shard_map(
        on_device,
        mesh=mesh,
        in_specs=(
            P("aa", "ba", "col", None),
            P("aa", "ba", "col", None),
            P(),
            P(),
            P(),
            P(),
            P(),
            P("aa", "ba", "col"),
            P("aa", "ba", "col"),
            P("aa", "ba", "col"),
        ),
        out_specs=(P("aa", "ba", "col", None), P("aa", "ba", "col", None), P(), P(), P(), P(), P()),
        check_vma=False,
    )
```

profile of v0, /device:TPU:0, one launch (start us, length us, event | category | flops | bytes accessed | tf_op | source)
XLA Modules:
  0.0 1391.2 jit_solution(7911083347783548005)
XLA Ops:
  20.5 5.3 convolution_multiply_fusion
  36.7 44.8 %all-to-all-done.4 = f32[16,32,16,128]{3,2,0,1:T(8,128)} async-done(((f32[16,32,16,128]{3,2,0,1:T(8,128)}), f32[16,32,16,128]{3,2,0,1:T(8,128)}, u32[]{:S(2)}, u32[]{:S(2)}) %all-to-all-start.4) | async-done | bytes 4194336 | tf_op jit(solution)/shard_map/all_to_all | solution.py:36
  103.6 46.6 %all-to-all-done.5 = f32[4,4,4,1,1,8,16,128]{7,6,5,1,2,4,3,0:T(8,128)} async-done(((f32[4,4,4,1,1,8,16,128]{7,6,5,1,2,4,3,0:T(8,128)}), f32[4,4,4,1,1,8,16,128]{7,6,5,1,2,4,3,0:T(8,128)}, u32[]{:S(2)}, u32[]{:S(2)}) %all-to-all-start.5) | async-done | bytes 4194336 | tf_op jit(solution)/shard_map/all_to_all | solution.py:50
  150.2 5.4 all-to-all-start.2
  161.2 5.3 all-to-all-start.6
  167.6 91.0 %all-to-all-done.6 = f32[1,4,4,1,4,8,16,128]{7,6,5,4,2,3,0,1:T(8,128)} async-done(((f32[1,4,4,1,4,8,16,128]{7,6,5,4,2,3,0,1:T(8,128)}), f32[1,4,4,1,4,8,16,128]{7,6,5,4,2,3,0,1:T(8,128)}, u32[]{:S(2)}, u32[]{:S(2)}) %all-to-all-start.6) | async-done | bytes 4194336 | tf_op jit(solution)/shard_map/all_to_all | solution.py:49
  263.0 8.3 fusion.2
  271.4 5.4 copy.167
  276.8 98.5 %all_to_all.267 = f32[1,4,128,16,128]{4,3,1,0,2:T(8,128)} all-to-all(f32[1,4,128,16,128]{4,3,1,0,2:T(8,128)} %copy.167), channel_id=1, replica_groups=mesh['aa'=4,'ba'=4,'col'=2] {'ba'}, dimensions={2} | all-to-all | bytes 8388608 | tf_op jit(solution)/shard_map/all_to_all | solution.py:71
  375.3 14.5 %copy.169 = f32[4,4,32,16,128]{2,3,1,0,4:T(8,128)} copy(f32[4,4,32,16,128]{4,3,1,2,0:T(8,128)} %bitcast.208) | data formatting | bytes 8388608 | tf_op jit(solution)/shard_map/all_to_all | solution.py:71
  389.8 16.7 %reshape.81 = f32[2,1,524288]{2,1,0:T(1,128)} reshape(f32[128,4,4,16,32]{4,3,2,1,0:T(8,128)} %bitcast.191) | data formatting | bytes 8388608
  406.5 54.0 %all_to_all.268 = f32[2,1,524288]{2,1,0:T(1,128)} all-to-all(f32[2,1,524288]{2,1,0:T(1,128)} %reshape.81), channel_id=1, replica_groups=mesh['aa'=4,'ba'=4,'col'=2] {'col'}, dimensions={0} | all-to-all | bytes 8388608 | tf_op jit(solution)/shard_map/all_to_all | solution.py:70
  460.5 16.5 %reduce.4 = f32[2,524288]{1,0:T(2,128)} reduce(f32[2,1,524288]{2,1,0:T(1,128)} %all_to_all.268, f32[]{:T(128)} %broadcast.16), dimensions={1}, to_apply=%all_to_all.222.reduce_sub_computation | reduce | bytes 8388612 | tf_op jit(solution)/shard_map/all_to_all | solution.py:70
  477.1 14.2 %reshape.82 = f32[128,4,4,16,32]{4,3,2,1,0:T(8,128)} reshape(f32[2,524288]{1,0:T(2,128)} %reduce.4) | data formatting | bytes 8388608
  491.3 15.7 %copy.170 = f32[4,4,32,16,2,64]{5,3,4,2,1,0:T(8,128)} copy(f32[4,4,32,16,2,64]{2,3,1,0,5,4:T(8,128)} %bitcast.192) | data formatting | bytes 8388608 | tf_op jit(solution)/shard_map/all_to_all | solution.py:70
  507.0 10.3 convolution_bitcast_fusion.1
  517.3 8.1 copy.243
  525.4 8.7 reshape.83
  534.1 53.3 %all_to_all.269 = f32[2,1,524288]{2,1,0:T(1,128)} all-to-all(f32[2,1,524288]{2,1,0:T(1,128)} %reshape.83), channel_id=1, replica_groups=mesh['aa'=4,'ba'=4,'col'=2] {'col'}, dimensions={0} | all-to-all | bytes 8388608 | tf_op jit(solution)/shard_map/all_to_all | solution.py:78
  587.4 16.5 %reduce.5 = f32[2,524288]{1,0:T(2,128)} reduce(f32[2,1,524288]{2,1,0:T(1,128)} %all_to_all.269, f32[]{:T(128)} %broadcast.16), dimensions={1}, to_apply=%all_to_all.226.reduce_sub_computation | reduce | bytes 8388612 | tf_op jit(solution)/shard_map/all_to_all | solution.py:78
  603.9 10.0 reshape.84
  613.9 15.4 %copy.242 = f32[4,4,32,2,16,64]{5,3,4,2,1,0:T(2,128)} copy(f32[4,4,32,2,16,64]{5,2,1,0,4,3:T(8,128)} %bitcast.204) | data formatting | bytes 8388608 | tf_op jit(solution)/shard_map/all_to_all | solution.py:78
  629.3 9.0 reshape.55
  638.3 9.5 fusion.41
  647.7 14.4 %copy.173 = f32[4,4,32,16,128]{2,3,1,0,4:T(8,128)} copy(f32[4,4,32,16,128]{4,3,2,1,0:T(8,128)} %bitcast.211) | data formatting | bytes 8388608 | tf_op jit(solution)/shard_map/reshape | solution.py:84
  662.1 16.7 %reshape.85 = f32[2,1,524288]{2,1,0:T(1,128)} reshape(f32[128,4,4,16,32]{4,3,2,1,0:T(8,128)} %bitcast.193) | data formatting | bytes 8388608
  678.8 52.2 %all_to_all.270 = f32[2,1,524288]{2,1,0:T(1,128)} all-to-all(f32[2,1,524288]{2,1,0:T(1,128)} %reshape.85), channel_id=1, replica_groups=mesh['aa'=4,'ba'=4,'col'=2] {'col'}, dimensions={0} | all-to-all | bytes 8388608 | tf_op jit(solution)/shard_map/all_to_all | solution.py:85
  731.0 16.5 %reduce.6 = f32[2,524288]{1,0:T(2,128)} reduce(f32[2,1,524288]{2,1,0:T(1,128)} %all_to_all.270, f32[]{:T(128)} %broadcast.16), dimensions={1}, to_apply=%all_to_all.229.reduce_sub_computation | reduce | bytes 8388612 | tf_op jit(solution)/shard_map/all_to_all | solution.py:85
  747.5 14.2 %reshape.86 = f32[128,4,4,16,32]{4,3,2,1,0:T(8,128)} reshape(f32[2,524288]{1,0:T(2,128)} %reduce.6) | data formatting | bytes 8388608
  761.8 15.7 %copy.174 = f32[4,4,32,16,2,64]{5,3,4,2,1,0:T(8,128)} copy(f32[4,4,32,16,2,64]{2,3,1,0,5,4:T(8,128)} %bitcast.194) | data formatting | bytes 8388608 | tf_op jit(solution)/shard_map/all_to_all | solution.py:85
  777.4 12.0 convolution_bitcast_fusion
  789.5 8.6 reshape.87
  798.1 95.1 %all_to_all.271 = f32[4,1,262144]{2,1,0:T(1,128)} all-to-all(f32[4,1,262144]{2,1,0:T(1,128)} %reshape.87), channel_id=1, replica_groups=mesh['aa'=4,'ba'=4,'col'=2] {'ba'}, dimensions={0} | all-to-all | bytes 8388608 | tf_op jit(solution)/shard_map/all_to_all | solution.py:89
  893.2 15.3 %reduce.7 = f32[4,262144]{1,0:T(4,128)} reduce(f32[4,1,262144]{2,1,0:T(1,128)} %all_to_all.271, f32[]{:T(128)} %broadcast.16), dimensions={1}, to_apply=%all_to_all.233.reduce_sub_computation | reduce | bytes 8388612 | tf_op jit(solution)/shard_map/all_to_all | solution.py:89
  908.5 9.3 reshape.88
  917.7 8.0 copy.176
  925.7 6.8 copy.177
  932.5 49.2 %all_to_all.272 = f32[1,4,128,32,64]{2,4,1,0,3:T(8,128)S(1)} all-to-all(f32[1,4,128,32,64]{2,4,1,0,3:T(8,128)} %copy.177), channel_id=1, replica_groups=mesh['aa'=4,'ba'=4,'col'=2] {'col'}, dimensions={3} | all-to-all | bytes 8388608 | tf_op jit(solution)/shard_map/all_to_all | solution.py:88
  990.0 50.7 %all_to_all.273 = f32[1,1,4,4,4,8,16,128]{7,2,3,6,5,1,0,4:T(4,128)S(1)} all-to-all(f32[1,1,4,4,4,8,16,128]{7,2,3,6,5,1,0,4:T(4,128)S(1)} %copy.182), channel_id=1, replica_groups=mesh['aa'=4,'ba'=4,'col'=2] {'aa'}, dimensions={4} | all-to-all | bytes 8388608 | tf_op jit(solution)/shard_map/all_to_all | solution.py:102
  1042.0 96.1 %all_to_all.274 = f32[4,1,4,4,1,8,16,128]{7,2,0,6,5,4,1,3:T(4,128)S(1)} all-to-all(f32[4,1,4,4,1,8,16,128]{7,2,0,6,5,4,1,3:T(4,128)S(1)} %copy.183), channel_id=1, replica_groups=mesh['aa'=4,'ba'=4,'col'=2] {'ba'}, dimensions={3} | all-to-all | bytes 8388608 | tf_op jit(solution)/shard_map/all_to_all | solution.py:101
  1154.1 13.7 convolution_bitcast_fusion.3
  1167.8 11.4 convolution_bitcast_fusion.4
  1179.2 6.4 fusion.17
  1189.4 43.9 %all-reduce = (f32[64,64]{1,0:T(8,128)S(1)}, f32[32,32]{1,0:T(8,128)S(1)}) all-reduce(f32[64,64]{1,0:T(8,128)S(1)} %fusion.25, f32[32,32]{1,0:T(8,128)S(1)} %convolution_bitcast_fusion.4), channel_id=1, replica_groups=mesh['aa'=4,'ba'=4,'col'=2] {'aa','ba','col'}, use_global_device_ids=true, to_apply=%region_2.0 | all-reduce | flops 5120 | bytes 40960 | tf_op jit(solution)/shard_map/psum | solution.py:119
  1239.3 9.1 fusion.22
  1248.4 6.7 fusion.11
  1255.1 9.1 convolution_add_fusion
  1264.2 116.1 %all-reduce.4.cloned.1.call-done = (f32[128,128]{0,1:T(8,128)}, f32[128,128]{0,1:T(8,128)}, f32[128,128]{0,1:T(8,128)}) async-done(((f32[128,128]{0,1:T(8,128)}, f32[128,128]{0,1:T(8,128)}, f32[128,128]{0,1:T(8,128)}), (f32[128,128]{0,1:T(8,128)}, f32[128,128]{0,1:T(8,128)}, f32[128,128]{0,1:T(8,128)})) %all-reduce.4.cloned.1.call-update) | async-done | bytes 196624 | tf_op jit(solution)/shard_map/psum | solution.py:119
  (100 shorter events, 96.2 us)
Async XLA Ops:
  7.2 631.1 %copy-start = (f32[128,128]{1,0:T(8,128)S(1)}, f32[128,128]{1,0:T(8,128)}, u32[]{:S(2)}) copy-start(f32[128,128]{1,0:T(8,128)} %param.12) | copy-start | bytes 196612
  9.1 8.2 all-to-all-start
  16.1 9.7 copy-start.11
  17.2 11.2 all-to-all-start.3
  28.4 53.1 %all-to-all-start.4 = ((f32[16,32,16,128]{3,2,0,1:T(8,128)}), f32[16,32,16,128]{3,2,0,1:T(8,128)}, u32[]{:S(2)}, u32[]{:S(2)}) async-start(f32[16,32,16,128]{3,2,0,1:T(8,128)} %copy.161), calls=%async_computation.4 | async-start | bytes 8388608 | tf_op jit(solution)/shard_map/all_to_all | solution.py:36
  36.7 51.5 %copy-start.13 = (f32[64,8,16]{0,2,1:T(8,128)}, f32[64,8,16]{0,2,1:T(8,128)S(1)}, u32[]{:S(2)}) copy-start(f32[64,8,16]{0,2,1:T(8,128)S(1)} %mul.84) | copy-start | bytes 98308
  81.5 15.6 %all-to-all-start.1 = ((f32[4,1,2048]{2,1,0:T(1,128)}), f32[4,1,2048]{2,1,0:T(1,128)S(1)}, u32[]{:S(2)}, u32[]{:S(2)}) async-start(f32[4,1,2048]{2,1,0:T(1,128)} %reshape.77), calls=%async_computation.1 | async-start | bytes 65536 | tf_op jit(solution)/shard_map/all_to_all | solution.py:57
  84.8 3.5 copy-start.17
  88.2 4.4 copy-start.1
  97.1 53.1 %all-to-all-start.5 = ((f32[4,4,4,1,1,8,16,128]{7,6,5,1,2,4,3,0:T(8,128)}), f32[4,4,4,1,1,8,16,128]{7,6,5,1,2,4,3,0:T(8,128)}, u32[]{:S(2)}, u32[]{:S(2)}) async-start(f32[4,4,4,1,1,8,16,128]{7,6,5,1,2,4,3,0:T(8,128)} %copy.163), calls=%async_computation.5 | async-start | bytes 8388608 | tf_op jit(solution)/shard_map/all_to_all | solution.py:50
  150.2 11.0 all-to-all-start.2
  161.2 97.4 %all-to-all-start.6 = ((f32[1,4,4,1,4,8,16,128]{7,6,5,4,2,3,0,1:T(8,128)}), f32[1,4,4,1,4,8,16,128]{7,6,5,4,2,3,0,1:T(8,128)}, u32[]{:S(2)}, u32[]{:S(2)}) async-start(f32[1,4,4,1,4,8,16,128]{7,6,5,4,2,3,0,1:T(8,128)} %copy.164), calls=%async_computation.6 | async-start | bytes 8388608 | tf_op jit(solution)/shard_map/all_to_all | solution.py:49
  167.6 95.5 %copy-start.15 = (f32[128,128]{1,0:T(8,128)S(1)}, f32[128,128]{1,0:T(8,128)}, u32[]{:S(2)}) copy-start(f32[128,128]{1,0:T(8,128)} %param.15) | copy-start | bytes 196612
  261.1 2.0 copy-start.3
  491.3 15.7 %copy-start.19 = (f32[32,32]{1,0:T(8,128)S(1)}, f32[32,32]{1,0:T(8,128)}, u32[]{:S(2)}) copy-start(f32[32,32]{1,0:T(8,128)} %param.16) | copy-start | bytes 12292
  982.9 4.4 copy-start.5
  1138.1 1.2 copy-start.14
  1138.1 1.2 copy-start.18
  1139.3 5.2 copy-start.7
  1148.9 85.7 %all-to-all-start.15 = ((f32[64,8,16,128]{3,2,1,0:T(8,128)}), f32[64,8,16,128]{3,2,1,0:T(8,128)}, u32[]{:S(2)}, u32[]{:S(2)}) async-start(f32[64,8,16,128]{3,2,1,0:T(8,128)} %copy.186), calls=%async_computation.15 | async-start | bytes 8388608 | tf_op jit(solution)/shard_map/all_to_all | solution.py:112
  1153.8 226.4 %all-reduce.4.cloned.1.call-start = ((), (), s32[]{:S(2)}) async-start(), calls=%async_computation.16 | async-start | bytes 393216 | tf_op jit(solution)/shard_map/psum | solution.py:119
  1167.8 11.4 copy-start.4
  1167.8 11.4 copy-start.6
  1179.2 6.4 copy-start.2
  1179.2 6.4 copy-start.8
  1234.6 4.7 copy-start.10
  1234.6 4.7 copy-start.12
  1237.3 2.0 copy-start.9
  1239.3 9.1 copy-start.16
Sparse Core Ops, SparseCore 0:
  1255.2 124.9 all-reduce.3
where the time goes:
time: 1400 us; the launch traced here: 1390 us
  blocking collectives  593 us (42%)
  waiting for transfers between devices  300 us (21%)
  local copies, waits for them, and re-layouts  256 us (18%)
  matrix products  120 us (9%)
  other arithmetic  70.8 us (5%)
  starting transfers between devices  36.2 us (3%)
  between operations  14.7 us (1%)
    psum x1, waiting for transfers between devices, on_device(): lax.psum((raw_gate, raw_value, raw_first, raw_columns, raw_third), ('aa',...  116 us
    unnamed x63, local copies, waits for them, and re-layouts  111 us
    all_to_all x1, blocking collectives, on_device(): lax.all_to_all(third_in, 'ba', split_axis=2, concat_axis=0, tiled=True)  98.5 us
    all_to_all x1, blocking collectives, on_device(): lax.all_to_all(lax.all_to_all(grad_split_second, 'aa', split_axis=4, conc...  96.1 us
    all_to_all x1, blocking collectives, on_device(): lax.all_to_all(grad_third_in, 'ba', split_axis=0, concat_axis=2, tiled=True)  95.1 us
    all_to_all x1, waiting for transfers between devices, on_device(): lax.all_to_all(lax.all_to_all(split_values, 'aa', split_axis=0, concat_ax...  91 us
    all_to_all x1, blocking collectives, on_device(): lax.all_to_all(lax.all_to_all(third_in, 'ba', split_axis=2, concat_axis=0...  54 us
    all_to_all x1, blocking collectives, on_device(): lax.all_to_all(mixed_third, 'col', split_axis=3, concat_axis=4, tiled=True)  53.3 us
  transfers between devices with their start and end apart: 9, of which 6 were waited for; matrix products, arithmetic and copies ran while one was open for 6% of the time, Pallas kernels for 0%

commit v1 on v0

v1 whole, which is shorter than its diff:
```python
import functools

import jax
import jax.numpy as jnp
from jax import lax
from jax.experimental import pallas as pl
from jax.experimental.pallas import tpu as pltpu
from jax.sharding import PartitionSpec as P

F32 = jnp.float32
BF16 = jnp.bfloat16
MESH = pl.DeviceIdType.MESH
VMEM = pltpu.VMEM
LIMIT = 56 * 1024 * 1024
SUB = 8


def split(x):
    hi = x.astype(BF16)
    return hi, (x - hi.astype(F32)).astype(BF16)


def split_weight(x):
    hi = lax.reduce_precision(x, 8, 7)
    return hi.astype(BF16), (x - hi).astype(BF16)


def dot(a, b, dims=((1,), (0,))):
    return lax.dot_general(a, b, (dims, ((), ())), preferred_element_type=F32)


def dot3(a, b, dims=((1,), (0,))):
    return dot(a[0], b[0], dims) + (dot(a[0], b[1], dims) + dot(a[1], b[0], dims))


NT = ((1,), (1,))
TN = ((0,), (0,))


def expand(m, inner):
    n = m.shape[0]
    row = lax.broadcasted_iota(jnp.int32, (n * SUB, n * SUB), 0)
    col = lax.broadcasted_iota(jnp.int32, (n * SUB, n * SUB), 1)
    at = lax.broadcasted_iota(jnp.int32, (n * SUB, n), 0)
    place = at // SUB if inner else at % n
    pick = (place == lax.broadcasted_iota(jnp.int32, (n * SUB, n), 1)).astype(F32)
    highest = lax.Precision.HIGHEST
    spread = jnp.dot(jnp.dot(pick, m, precision=highest), pick.T, precision=highest)
    kept = row % SUB == col % SUB if inner else row // n == col // n
    return jnp.where(kept, spread, 0.0)


def coords():
    return {n: lax.axis_index(n) for n in ("aa", "ba", "col")}


def sizes():
    return {n: lax.axis_size(n) for n in ("aa", "ba", "col")}


def peers(axes, size):
    me = coords()
    total = 1
    mine = 0
    for n in axes:
        mine = mine * size[n] + me[n]
        total *= size[n]
    found = []
    for step in range(total):
        at = lax.rem(mine + step, total)
        there = dict(me)
        for n in reversed(axes):
            there[n] = lax.rem(at, size[n])
            at = at // size[n]
        found.append(there)
    return found


def barrier(groups, size):
    sem = pltpu.get_barrier_semaphore()
    count = 0
    for axes, skip in groups:
        for step, there in enumerate(peers(axes, size)):
            if step == 0 or (skip is not None and skip(step)):
                continue
            pl.semaphore_signal(sem, inc=1, device_id=there, device_id_type=MESH)
            count += 1
    pl.semaphore_wait(sem, count)


def send(axes, size, source, target, send_sem, recv_sem):
    me = coords()
    copies = []
    for step, there in enumerate(peers(axes, size)):
        if step == 0:
            copy = pltpu.make_async_copy(source(there), target(me), send_sem.at[0])
        else:
            copy = pltpu.make_async_remote_copy(
                src_ref=source(there),
                dst_ref=target(me),
                send_sem=send_sem.at[step],
                recv_sem=recv_sem.at[step],
                device_id=there,
                device_id_type=MESH,
            )
        copy.start()
        copies.append(copy)
    return copies


def finish(*groups):
    for copies in groups:
        for copy in copies:
            copy.wait()


def block(index, width):
    return pl.ds(pl.multiple_of(index * width, width), width)


def lanes(parts):
    return parts[0] if len(parts) == 1 else jnp.concatenate(parts, axis=1)


def gather_first(ref, j):
    n, _, k, c = ref.shape
    return lanes([ref[:, j, t * SUB:(t + 1) * SUB, :].reshape(n * SUB, c) for t in range(k // SUB)])


def scatter_first(ref, j, value):
    n, _, k, c = ref.shape
    for t in range(k // SUB):
        ref[:, j, t * SUB:(t + 1) * SUB, :] = value[:, t * c:(t + 1) * c].reshape(n, SUB, c)


def gather_second(ref, i):
    _, n, k, c = ref.shape
    return lanes([ref[i, :, t * SUB:(t + 1) * SUB, :].reshape(n * SUB, c) for t in range(k // SUB)])


def scatter_second(ref, i, value):
    _, n, k, c = ref.shape
    for t in range(k // SUB):
        ref[i, :, t * SUB:(t + 1) * SUB, :] = value[:, t * c:(t + 1) * c].reshape(n, SUB, c)


def gather_third(ref, i):
    _, r, k, c = ref.shape
    return lanes([ref[i, t * SUB:(t + 1) * SUB, :, :].reshape(SUB * k, c) for t in range(r // SUB)])


def scatter_third(ref, i, value):
    _, r, k, c = ref.shape
    for t in range(r // SUB):
        ref[i, t * SUB:(t + 1) * SUB, :, :] = value[:, t * c:(t + 1) * c].reshape(SUB, k, c)


def loop(count, body):
    def step(i, carry):
        body(i)
        return carry

    lax.fori_loop(0, count, step, 0)


def fold_inner(p, n):
    rows = lax.broadcasted_iota(jnp.int32, p.shape, 0)
    cols = lax.broadcasted_iota(jnp.int32, p.shape, 1)
    kept = jnp.where(lax.rem(rows, SUB) == lax.rem(cols, SUB), p, 0.0)
    summed = jnp.sum(kept.reshape(n, SUB, n * SUB), axis=1)
    pick = (
        lax.broadcasted_iota(jnp.int32, (n * SUB, n), 0) // SUB
        == lax.broadcasted_iota(jnp.int32, (n * SUB, n), 1)
    ).astype(F32)
    return jnp.dot(summed, pick, precision=lax.Precision.HIGHEST, preferred_element_type=F32)


def fold_outer(p, n):
    rows = lax.broadcasted_iota(jnp.int32, p.shape, 0)
    cols = lax.broadcasted_iota(jnp.int32, p.shape, 1)
    kept = jnp.where(rows // n == cols // n, p, 0.0)
    summed = jnp.sum(kept.reshape(SUB, n, n * SUB), axis=0)
    pick = (
        lax.rem(lax.broadcasted_iota(jnp.int32, (n * SUB, n), 0), n)
        == lax.broadcasted_iota(jnp.int32, (n * SUB, n), 1)
    ).astype(F32)
    return jnp.dot(summed, pick, precision=lax.Precision.HIGHEST, preferred_element_type=F32)


def kernel_one(size, x_ref, cot_ref, wh_ref, wl_ref, tw1_ref, tw2_ref, tw3_ref,
               f1_ref, g3_ref, sig_ref, t2_ref, t3_ref, s_buf, g_buf,
               sa, ra, sc, rc, s2, r2, s3, r3):
    h1, h2, h3, c = x_ref.shape
    q = f1_ref.shape[1]
    r = g3_ref.shape[1]
    barrier([(("aa",), None), (("ba",), None), (("col",), None)], size)
    tw2 = send(("aa",), size, lambda t: tw2_ref.at[t["aa"]], lambda m: t2_ref.at[m["aa"]], s2, r2)
    tw3 = send(("ba",), size, lambda t: tw3_ref.at[t["ba"]], lambda m: t3_ref.at[m["ba"]], s3, r3)

    def work(i):
        both = dot3(split(x_ref[i].reshape(h2 * h3, c)), (wh_ref[...], wl_ref[...]))
        sig = jax.nn.sigmoid(both[:, :c]).reshape(h2, h3, c)
        sig_ref[i] = sig
        g_buf[i] = cot_ref[i] * sig
        s_buf[i] = tw1_ref[i] * both[:, c:].reshape(h2, h3, c)

    loop(h1, work)
    first = send(("aa",), size, lambda t: s_buf.at[:, block(t["aa"], q)],
                 lambda m: f1_ref.at[block(m["aa"], h1)], sa, ra)
    third = send(("col",), size, lambda t: g_buf.at[:, block(t["col"], r)],
                 lambda m: g3_ref.at[:, :, block(m["col"], h3), :], sc, rc)
    finish(tw2, tw3, first, third)


def greet(size):
    sem = pltpu.get_barrier_semaphore()
    me = coords()
    count = 0
    for there in peers(("aa", "ba"), size)[1:]:
        pl.semaphore_signal(sem, inc=1, device_id=there, device_id_type=MESH)
        count += 1
    for step in range(1, size["col"]):
        col = lax.rem(me["col"] + step, size["col"])
        for other in range(size["ba"]):
            there = {"aa": me["aa"], "ba": lax.rem(me["ba"] + other, size["ba"]), "col": col}
            pl.semaphore_signal(sem, inc=1, device_id=there, device_id_type=MESH)
            count += 1
    pl.semaphore_wait(sem, count)


def kernel_two(size, f1_ref, g3_ref, m1h, m1l, m3h, m3l, tw2_ref, f2_ref, g2_ref,
               s_buf, g_buf, sa, ra, sb, rb):
    n1, q, h3, c = f1_ref.shape
    h1, r, n3, _ = g3_ref.shape
    p = f2_ref.shape[0]
    h2 = r * size["col"]
    greet(size)

    def mix_first(j):
        out = dot3((m1h[...], m1l[...]), split(gather_first(f1_ref, j)))
        scatter_first(s_buf, j, out * gather_first(tw2_ref, j))

    loop(q, mix_first)
    fwd = send(("aa", "ba"), size, lambda t: s_buf.at[block(t["aa"] * size["ba"] + t["ba"], p)],
               lambda m: f2_ref.at[:, block(m["ba"] * size["aa"] + m["aa"], q)], sa, ra)

    def back_third(i):
        scatter_third(g_buf, i, dot3((m3h[...], m3l[...]), split(gather_third(g3_ref, i))))

    loop(h1, back_third)
    bwd = send(("ba", "col"), size,
               lambda t: g_buf.at[block(t["ba"], p), :, block(t["col"], h3), :],
               lambda m: g2_ref.at[:, block(m["ba"] * size["col"] + m["col"], r)], sb, rb)
    finish(fwd, bwd)


def kernel_three(size, f2_ref, g2_ref, m2h, m2l, m2th, m2tl, tw3_ref, f3_ref, g1_ref, raw_ref,
                 s_buf, g_buf, acc, sa, ra, sb, rb):
    p, n2, h3, c = f2_ref.shape
    r = f3_ref.shape[1]
    q = g1_ref.shape[1]
    h2 = r * size["col"]
    greet(size)

    def mix_second(i):
        out = dot3((m2h[...], m2l[...]), split(gather_second(f2_ref, i)))
        scatter_second(s_buf, i, out * gather_second(tw3_ref, i))

    loop(p, mix_second)
    fwd = send(("ba", "col"), size,
               lambda t: s_buf.at[:, block(t["ba"] * size["col"] + t["col"], r)],
               lambda m: f3_ref.at[block(m["ba"], p), :, block(m["col"], h3), :], sb, rb)

    def back_second(i):
        grad = gather_second(tw3_ref, i) * gather_second(g2_ref, i)
        scatter_second(g_buf, i, dot3((m2th[...], m2tl[...]), split(grad)))

    loop(p, back_second)
    bwd = send(("aa", "ba"), size,
               lambda t: g_buf.at[:, block(t["ba"] * size["aa"] + t["aa"], q)],
               lambda m: g1_ref.at[block(m["aa"] * size["ba"] + m["ba"], p)], sa, ra)

    acc[...] = jnp.zeros_like(acc)

    def raw(i):
        ahead = split(gather_second(f2_ref, i))
        grad = split(gather_second(tw3_ref, i) * gather_second(g2_ref, i))
        for s in range(0, n2 * SUB, 128):
            acc[s:s + 128, :] += dot3((grad[0][s:s + 128], grad[1][s:s + 128]), ahead, NT)

    loop(p, raw)
    raw_ref[...] = fold_inner(acc[...], n2)
    finish(fwd, bwd)


def kernel_four(size, f3_ref, g1_ref, f1_ref, g3_ref, m3h, m3l, m1h, m1l, tw2_ref,
                mixed_ref, g0_ref, raw1_ref, raw3_ref, s_buf, g_buf, acc1, acc3,
                sa, ra, sb, rb):
    h1, r, n3, c = f3_ref.shape
    n1, q, h3, _ = f1_ref.shape
    barrier([(("aa",), None), (("col",), None)], size)

    def mix_third(i):
        scatter_third(s_buf, i, dot3((m3h[...], m3l[...]), split(gather_third(f3_ref, i))))

    loop(h1, mix_third)
    fwd = send(("col",), size, lambda t: s_buf.at[:, :, block(t["col"], h3), :],
               lambda m: mixed_ref.at[:, block(m["col"], r)], sb, rb)

    def back_first(j):
        grad = gather_first(tw2_ref, j) * gather_first(g1_ref, j)
        scatter_first(g_buf, j, dot3((m1h[...], m1l[...]), split(grad)))

    loop(q, back_first)
    bwd = send(("aa",), size, lambda t: g_buf.at[block(t["aa"], h1)],
               lambda m: g0_ref.at[:, block(m["aa"], q)], sa, ra)

    acc1[...] = jnp.zeros_like(acc1)
    acc3[...] = jnp.zeros_like(acc3)

    def raw_first(j):
        ahead = split(gather_first(f1_ref, j))
        grad = split(gather_first(tw2_ref, j) * gather_first(g1_ref, j))
        for s in range(0, n1 * SUB, 128):
            acc1[s:s + 128, :] += dot3((grad[0][s:s + 128], grad[1][s:s + 128]), ahead, NT)

    loop(q, raw_first)

    def raw_third(i):
        acc3[...] += dot3(split(gather_third(g3_ref, i)), split(gather_third(f3_ref, i)), NT)

    loop(h1, raw_third)
    raw1_ref[...] = fold_inner(acc1[...], n1)
    raw3_ref[...] = fold_outer(acc3[...], n3)
    finish(fwd, bwd)


def kernel_five(x_ref, cot_ref, sig_ref, mixed_ref, g0_ref, tw1_ref, wh_ref, wl_ref,
                out_ref, gin_ref, rg_ref, rv_ref):
    _, h2, h3, c = x_ref.shape
    rows = h2 * h3

    @pl.when(pl.program_id(0) == 0)
    def _():
        rg_ref[...] = jnp.zeros_like(rg_ref)
        rv_ref[...] = jnp.zeros_like(rv_ref)

    sig = sig_ref[0].reshape(rows, c)
    out = sig * mixed_ref[0].reshape(rows, c)
    out_ref[0] = out.reshape(h2, h3, c)
    gate = cot_ref[0].reshape(rows, c) * out * (1.0 - sig)
    value = tw1_ref[0].reshape(rows, c) * g0_ref[0].reshape(rows, c)
    both = split(jnp.concatenate([gate, value], axis=1))
    gin = dot3(both, (wh_ref[...], wl_ref[...]), NT)
    gin_ref[0] = gin.reshape(h2, h3, c)
    raw = dot3(split(x_ref[0].reshape(rows, c)), both, TN)
    rg_ref[...] += raw[:, :c]
    rv_ref[...] += raw[:, c:]


def kernel_sum(size, factor, part_ref, out_ref, land, total, sa, ra, sb, rb):
    axes = ("aa", "ba", "col")
    n, ch, _ = part_ref.shape
    barrier([(axes, None)], size)

    def index(t):
        return (t["aa"] * size["ba"] + t["ba"]) * size["col"] + t["col"]

    finish(send(axes, size, lambda t: part_ref.at[index(t)], lambda m: land.at[index(m)], sa, ra))
    total[...] = jnp.sum(land[...], axis=0) * factor
    finish(send(axes, size, lambda t: total, lambda m: out_ref.at[index(m)], sb, rb))


def sems(*counts):
    return [pltpu.SemaphoreType.DMA((n,)) for n in counts for _ in range(2)]


def on_device(inputs, cotangent, w_gate, w_value, mix_first, mix_second, mix_third,
              twiddle_first, twiddle_second, twiddle_third):
    size = sizes()
    na, nb, nc = size["aa"], size["ba"], size["col"]
    h1, h2, h3, c = inputs.shape
    n1, n2, n3 = mix_first.shape[0], mix_second.shape[0], mix_third.shape[0]
    p, q, r = n1 // (na * nb), n2 // (na * nb), h2 // nc
    any_ = pl.BlockSpec(memory_space=pl.ANY)
    vm = pl.BlockSpec(memory_space=VMEM)
    sds = lambda *s: jax.ShapeDtypeStruct(s, F32)
    home, l1, l2, l3 = (h1, h2, h3, c), (n1, q, h3, c), (p, n2, h3, c), (h1, r, n3, c)

    def call(body, cid, outs, out_specs, in_specs, scratch, *args):
        return pl.pallas_call(
            body,
            out_shape=outs,
            in_specs=in_specs,
            out_specs=out_specs,
            scratch_shapes=scratch,
            compiler_params=pltpu.CompilerParams(
                collective_id=cid, has_side_effects=True, vmem_limit_bytes=LIMIT
            ),
        )(*args)

    wide = lambda t: jnp.broadcast_to(t[..., None], t.shape + (c,))
    k1 = split_weight(expand(mix_first, True))
    k1t = split_weight(expand(mix_first.T, True))
    k2 = split_weight(expand(mix_second, True))
    k2t = split_weight(expand(mix_second.T, True))
    k3 = split_weight(expand(mix_third, False))
    k3t = split_weight(expand(mix_third.T, False))
    w = split_weight(jnp.concatenate([w_gate, w_value], axis=1))
    tw1 = wide(twiddle_first)
    tw2s = twiddle_second.reshape(h1, na, q * h3).transpose(1, 0, 2)
    tw3s = twiddle_third.reshape(nb, p, h2 * h3)

    f1, g3, sig, t2, t3 = call(
        functools.partial(kernel_one, size), 0,
        (sds(*l1), sds(*l3), sds(*home), sds(na, h1, q * h3), sds(nb, p, h2 * h3)),
        (any_, any_, vm, any_, any_), [vm] * 5 + [any_] * 2,
        [VMEM(home, F32), VMEM(home, F32)] + sems(na, nc, na, nb),
        inputs, cotangent, *w, tw1, tw2s, tw3s)
    tw2 = wide(t2.reshape(n1, q, h3))
    tw3 = wide(t3.reshape(nb, p, h2, h3).transpose(1, 0, 2, 3).reshape(p, n2, h3))

    f2, g2 = call(
        functools.partial(kernel_two, size), 1, (sds(*l2), sds(*l2)), (any_, any_), [vm] * 7,
        [VMEM(l1, F32), VMEM(l3, F32)] + sems(na * nb, nb * nc),
        f1, g3, *k1, *k3t, tw2)

    f3, g1, raw2 = call(
        functools.partial(kernel_three, size), 2, (sds(*l3), sds(*l1), sds(n2, n2)),
        (any_, any_, vm), [vm] * 7,
        [VMEM(l2, F32), VMEM(l2, F32), VMEM((n2 * SUB, n2 * SUB), F32)] + sems(na * nb, nb * nc),
        f2, g2, *k2, *k2t, tw3)

    mixed, g0, raw1, raw3 = call(
        functools.partial(kernel_four, size), 3,
        (sds(*home), sds(*home), sds(n1, n1), sds(n3, n3)),
        (any_, any_, vm, vm), [vm] * 9,
        [VMEM(l3, F32), VMEM(l1, F32), VMEM((n1 * SUB, n1 * SUB), F32),
         VMEM((n3 * SUB, n3 * SUB), F32)] + sems(na, nc),
        f3, g1, f1, g3, *k3, *k1t, tw2)

    row = pl.BlockSpec((1, h2, h3, c), lambda i: (i, 0, 0, 0))
    whole = lambda *s: pl.BlockSpec(s, lambda i: (0,) * len(s))
    output, grad_inputs, raw_gate, raw_value = pl.pallas_call(
        kernel_five,
        grid=(h1,),
        out_shape=(sds(*home), sds(*home), sds(c, c), sds(c, c)),
        in_specs=[row] * 6 + [whole(c, 2 * c)] * 2,
        out_specs=(row, row, whole(c, c), whole(c, c)),
        compiler_params=pltpu.CompilerParams(vmem_limit_bytes=LIMIT),
    )(inputs, cotangent, sig, mixed, g0, tw1, *w)

    flat = jnp.concatenate([t.reshape(-1) for t in (raw_gate, raw_value, raw2, raw1, raw3)])
    n = na * nb * nc
    unit = n * SUB * 128
    padded = -(-flat.shape[0] // unit) * unit
    parts = jnp.pad(flat, (0, padded - flat.shape[0])).reshape(n, -1, 128)
    factor = float(n1 * n2 * n3) ** (-0.5)
    summed = call(
        functools.partial(kernel_sum, size, factor), 4, sds(*parts.shape), vm, [vm],
        [VMEM(parts.shape, F32), VMEM(parts.shape[1:], F32)] + sems(n, n), parts).reshape(-1)
    at = 0
    order = ((c, c), (c, c), (n2, n2), (n1, n1), (n3, n3))
    taken = []
    for shape in order:
        span = shape[0] * shape[1]
        taken.append(summed[at:at + span].reshape(shape))
        at += span
    return output, grad_inputs, taken[0], taken[1], taken[3], taken[2], taken[4]


def solution(mesh):
    cut = P("aa", "ba", "col", None)
    narrow = P("aa", "ba", "col")
    return jax.shard_map(
        on_device,
        mesh=mesh,
        in_specs=(cut, cut, P(), P(), P(), P(), P(), narrow, narrow, narrow),
        out_specs=(cut, cut, P(), P(), P(), P(), P()),
        check_vma=False,
    )
```

time: 1400 us -> 609 us (0.43)
  blocking collectives: 593 us -> 0 us
  Pallas kernels: 0 us -> 564 us
  waiting for transfers between devices: 300 us -> 0 us
  local copies, waits for them, and re-layouts: 256 us -> 20.9 us
  matrix products: 120 us -> 21.3 us
  other arithmetic: 70.8 us -> 0.72 us
  starting transfers between devices: 36.2 us -> 0 us
    pallas_call x0 -> x6, Pallas kernels: none -> 564 us  [the longest x5 546 us: call(): pl.pallas_call(body, out_shape=outs, in_specs=in_specs, out_specs=out_spe...]
    all_to_all x8 -> x0, blocking collectives: 549 us -> none  [the longest x1 98.5 us: on_device(): lax.all_to_all(third_in, 'ba', split_axis=2, concat_axis=0, tiled=True)]
    all_to_all x8 -> x0, waiting for transfers between devices: 184 us -> none  [the longest x1 91 us: on_device(): lax.all_to_all(lax.all_to_all(split_values, 'aa', split_axis=0, concat_ax...]
    psum x1 -> x0, waiting for transfers between devices: 116 us -> none  [on_device(): lax.psum((raw_gate, raw_value, raw_first, raw_columns, raw_third), ('aa',...]
    unnamed x63 -> x28, local copies, waits for them, and re-layouts: 111 us -> 3.92 us
    dot_general x15 -> x12, matrix products: 120 us -> 21.3 us  [the longest x6 15.7 us: expand(): jnp.dot(jnp.dot(pick, m, precision=highest), pick.T, precision=highest)]
    all_to_all x19 -> x0, local copies, waits for them, and re-layouts: 93.6 us -> none  [the longest x1 15.7 us: on_device(): lax.all_to_all(lax.all_to_all(third_in, 'ba', split_axis=2, concat_axis=0...]
    all_to_all x8 -> x0, other arithmetic: 67.8 us -> none  [the longest x1 16.5 us: on_device(): lax.all_to_all(mixed_third, 'col', split_axis=3, concat_axis=4, tiled=True)]
  transfers between devices with their start and end apart: 9 -> 0, of which waited for: 6 -> 0; matrix products, arithmetic and copies ran while one was open for 6% -> 0% of each run, Pallas kernels for 0% -> 0%
where the time goes in v1:
time: 609 us; the launch traced here: 608 us
  Pallas kernels  564 us (93%)
  matrix products  21.3 us (3%)
  local copies, waits for them, and re-layouts  20.9 us (3%)
    pallas_call x5, Pallas kernels, call(): pl.pallas_call(body, out_shape=outs, in_specs=in_specs, out_specs=out_spe...  546 us
    pallas_call x1, Pallas kernels, on_device(): pl.pallas_call(kernel_five, grid=(h1,), out_shape=(sds(*home), sds(*home)...  18.4 us
    dot_general x6, matrix products, expand(): jnp.dot(jnp.dot(pick, m, precision=highest), pick.T, precision=highest)  15.7 us

profile of v1, /device:TPU:0, one launch (start us, length us, event | category | flops | bytes accessed | tf_op | source)
XLA Modules:
  0.0 607.9 jit_solution(7506349251374542338)
XLA Ops:
  0.6 0.0 copy-start
  0.7 0.0 copy-start.2
  0.7 0.0 copy-start.3
  0.7 0.9 constant_dynamic-update-slice_fusion.1
  1.6 0.8 constant_dynamic-update-slice_fusion
  2.4 0.7 fusion.24
  3.1 1.0 copy.24
  4.1 2.6 broadcast_in_dim.35.tw1_ref
  6.7 0.1 copy.25
  6.8 0.1 reshape.68
  7.0 0.6 copy.33
  7.6 0.1 copy.27
  7.7 0.8 reshape.69.tw3_ref
  8.5 64.8 %shard_map.153 = (f32[64,8,16,128]{3,2,1,0:T(8,128)}, f32[16,16,32,128]{3,2,1,0:T(8,128)}, f32[16,32,16,128]{3,2,1,0:T(8,128)}, f32[4,16,128]{2,1,0:T(8,128)}, f32[4,4,512]{2,1,0:T(4,128)}) custom-call(f32[16,32,16,128]{3,2,1,0:T(8,128)} %x_ref.3, f32[16,32,16,128]{3,2,1,0:T(8,128)} %cot_ref.3, bf16[128,256]{1,0:T(8,128)(2,1)} %get-tuple-element.59.wh_ref, ...), custom_call_target="tpu_custom_call" | custom-call | tf_op jit(solution)/shard_map/pallas_call | solution.py:391
  73.4 0.9 fusion.19
  74.3 2.0 fusion.2
  76.3 0.3 fusion.26
  76.6 1.2 fusion.8
  77.9 0.9 broadcast_in_dim.38
  78.7 2.6 broadcast_in_dim.39.tw2_ref
  81.4 161.9 %shard_map.154 = (f32[4,128,16,128]{3,2,1,0:T(8,128)}, f32[4,128,16,128]{3,2,1,0:T(8,128)}) custom-call(f32[64,8,16,128]{3,2,1,0:T(8,128)} %get-tuple-element.26.f1_ref, f32[16,16,32,128]{3,2,1,0:T(8,128)} %get-tuple-element.27.g3_ref, bf16[512,512]{1,0:T(8,128)(2,1)} %get-tuple-element.50.m1h, bf16[512,512]{1,0:T(8,128)(2,1)} %get-tuple-element.49.m1l, ...), custom_call_target="tpu_custom_call" | custom-call | tf_op jit(solution)/shard_map/pallas_call | solution.py:391
  243.3 1.6 fusion.7
  244.9 2.8 fusion.6
  247.8 1.6 fusion.5
  249.4 0.0 copy-start.5
  249.4 6.5 %fusion.1 = (bf16[1024,1024]{1,0:T(8,128)(2,1)}, bf16[1024,1024]{1,0:T(8,128)(2,1)}, bf16[1024,1024]{1,0:T(8,128)(2,1)}, bf16[1024,1024]{1,0:T(8,128)(2,1)}) fusion(s32[1024]{0:T(1024)S(1)} %get-tuple-element.76, s32[1024]{0:T(1024)S(1)} %get-tuple-element.77, pred[1024]{0:T(1024)(128)(4,1)S(1)} %get-tuple-element.79, f32[1024,1024]{1,0:T(8,128)S(1)} %fusion.6, ...), kind=kOutput, calls=%fused_computation.5 | convolution fusion | flops 1624506368 | bytes 13125632 | tf_op jit(solution)/shard_map/dot_general | solution.py:48
  255.9 0.1 reshape.70
  256.0 2.6 broadcast_in_dim.42.tw3_ref
  258.7 227.1 %shard_map.155 = (f32[16,16,32,128]{3,2,1,0:T(8,128)}, f32[64,8,16,128]{3,2,1,0:T(8,128)}, f32[128,128]{1,0:T(8,128)}) custom-call(f32[4,128,16,128]{3,2,1,0:T(8,128)} %get-tuple-element.29.f2_ref, f32[4,128,16,128]{3,2,1,0:T(8,128)} %get-tuple-element.30.g2_ref, bf16[1024,1024]{1,0:T(8,128)(2,1)} %get-tuple-element.60.m2h, ...), custom_call_target="tpu_custom_call" | custom-call | tf_op jit(solution)/shard_map/pallas_call | solution.py:391
  485.8 0.3 fusion.25
  486.1 1.2 fusion.9
  487.3 0.9 fusion.18
  488.2 2.0 fusion.3
  490.1 63.5 %shard_map.156 = (f32[16,32,16,128]{3,2,1,0:T(8,128)}, f32[16,32,16,128]{3,2,1,0:T(8,128)}, f32[64,64]{1,0:T(8,128)}, f32[32,32]{1,0:T(8,128)}) custom-call(f32[16,16,32,128]{3,2,1,0:T(8,128)} %get-tuple-element.32.f3_ref, f32[64,8,16,128]{3,2,1,0:T(8,128)} %get-tuple-element.33.g1_ref, f32[64,8,16,128]{3,2,1,0:T(8,128)} %get-tuple-element.26.f1_ref, ...), custom_call_target="tpu_custom_call" | custom-call | tf_op jit(solution)/shard_map/pallas_call | solution.py:391
  553.7 0.0 copy-start.1
  553.7 18.4 %shard_map.157 = (f32[16,32,16,128]{3,2,1,0:T(8,128)}, f32[16,32,16,128]{3,2,1,0:T(8,128)}, f32[128,128]{1,0:T(8,128)}, f32[128,128]{1,0:T(8,128)}) custom-call(f32[16,32,16,128]{3,2,1,0:T(8,128)} %x_ref.3, f32[16,32,16,128]{3,2,1,0:T(8,128)} %cot_ref.3, f32[16,32,16,128]{3,2,1,0:T(8,128)} %get-tuple-element.25.sig_ref, ...), custom_call_target="tpu_custom_call" | custom-call | tf_op jit(solution)/shard_map/pallas_call | solution.py:444
  572.1 0.8 bitcast_dynamic-update-slice_fusion.2
  572.9 0.8 bitcast_dynamic-update-slice_fusion.1
  573.8 0.1 reshape.74
  573.9 0.1 reshape.75
  573.9 0.7 pad.4
  574.7 28.4 %shard_map.158 = f32[32,16,128]{2,1,0:T(8,128)} custom-call(f32[32,16,128]{2,1,0:T(8,128)} %bitcast.28), custom_call_target="tpu_custom_call" | custom-call | tf_op jit(solution)/shard_map/pallas_call | solution.py:391
  603.1 1.6 fusion.65
  604.6 0.7 slice.24
  605.4 0.7 reshape.79
  606.1 1.2 slice.26
  607.3 0.6 slice.28
  607.9 0.0 copy-done.1
  (27 shorter events, 0.1 us)
Async XLA Ops:
  0.6 242.7 %copy-start = (f32[128,128]{1,0:T(8,128)S(1)}, f32[128,128]{1,0:T(8,128)}, u32[]{:S(2)}) copy-start(f32[128,128]{1,0:T(8,128)} %param.15) | copy-start | bytes 196612
  0.7 6.0 copy-start.2
  0.7 6.9 %copy-start.3 = (f32[16,32,16]{1,2,0:T(8,128)S(1)}, f32[16,32,16]{1,2,0:T(8,128)}, u32[]{:S(2)}) copy-start(f32[16,32,16]{1,2,0:T(8,128)} %param.19) | copy-start | bytes 98308
  8.5 64.9 %copy-start.8 = (f32[64,64]{1,0:T(8,128)S(1)}, f32[64,64]{1,0:T(8,128)}, u32[]{:S(2)}) copy-start(f32[64,64]{1,0:T(8,128)} %param.14) | copy-start | bytes 49156
  8.5 67.8 %copy-start.9 = (f32[32,32]{1,0:T(8,128)S(1)}, f32[32,32]{1,0:T(8,128)}, u32[]{:S(2)}) copy-start(f32[32,32]{1,0:T(8,128)} %param.16) | copy-start | bytes 12292
  249.4 6.5 %copy-start.5 = (f32[4,4,512]{2,1,0:T(4,128)S(1)}, f32[4,4,512]{2,1,0:T(4,128)}, u32[]{:S(2)}) copy-start(f32[4,4,512]{2,1,0:T(4,128)} %get-tuple-element.31) | copy-start | bytes 98308
  553.6 20.1 %copy-start.4 = (f32[128,128]{1,0:T(8,128)S(1)}, f32[128,128]{1,0:T(8,128)}, u32[]{:S(2)}) copy-start(f32[128,128]{1,0:T(8,128)} %get-tuple-element.40) | copy-start | bytes 196612
  553.6 20.1 %copy-start.6 = (f32[64,64]{1,0:T(8,128)S(1)}, f32[64,64]{1,0:T(8,128)}, u32[]{:S(2)}) copy-start(f32[64,64]{1,0:T(8,128)} %get-tuple-element.41) | copy-start | bytes 49156
  553.7 20.2 %copy-start.7 = (f32[32,32]{1,0:T(8,128)S(1)}, f32[32,32]{1,0:T(8,128)}, u32[]{:S(2)}) copy-start(f32[32,32]{1,0:T(8,128)} %get-tuple-element.42) | copy-start | bytes 12292
  553.7 54.2 %copy-start.1 = (f32[128,128]{1,0:T(8,128)S(1)}, f32[128,128]{1,0:T(8,128)}, u32[]{:S(2)}) copy-start(f32[128,128]{1,0:T(8,128)} %param.15) | copy-start | bytes 196612

commit v2 on v1

--- a/solution.py
+++ b/solution.py
@@ -11,7 +11,7 @@
 BF16 = jnp.bfloat16
 MESH = pl.DeviceIdType.MESH
 VMEM = pltpu.VMEM
-LIMIT = 56 * 1024 * 1024
+LIMIT = 60 * 1024 * 1024
 SUB = 8
 
 
@@ -122,26 +122,9 @@
     return parts[0] if len(parts) == 1 else jnp.concatenate(parts, axis=1)
 
 
-def gather_first(ref, j):
-    n, _, k, c = ref.shape
-    return lanes([ref[:, j, t * SUB:(t + 1) * SUB, :].reshape(n * SUB, c) for t in range(k // SUB)])
-
-
-def scatter_first(ref, j, value):
-    n, _, k, c = ref.shape
-    for t in range(k // SUB):
-        ref[:, j, t * SUB:(t + 1) * SUB, :] = value[:, t * c:(t + 1) * c].reshape(n, SUB, c)
-
-
 def gather_second(ref, i):
     _, n, k, c = ref.shape
     return lanes([ref[i, :, t * SUB:(t + 1) * SUB, :].reshape(n * SUB, c) for t in range(k // SUB)])
-
-
-def scatter_second(ref, i, value):
-    _, n, k, c = ref.shape
-    for t in range(k // SUB):
-        ref[i, :, t * SUB:(t + 1) * SUB, :] = value[:, t * c:(t + 1) * c].reshape(n, SUB, c)
 
 
 def gather_third(ref, i):
@@ -188,12 +171,9 @@
 
 
 def kernel_one(size, x_ref, cot_ref, wh_ref, wl_ref, tw1_ref, tw2_ref, tw3_ref,
-               f1_ref, g3_ref, sig_ref, t2_ref, t3_ref, s_buf, g_buf,
-               sa, ra, sc, rc, s2, r2, s3, r3):
+               first_ref, grad_ref, sig_ref, t2_ref, t3_ref, s2, r2, s3, r3):
     h1, h2, h3, c = x_ref.shape
-    q = f1_ref.shape[1]
-    r = g3_ref.shape[1]
-    barrier([(("aa",), None), (("ba",), None), (("col",), None)], size)
+    barrier([(("aa",), None), (("ba",), None)], size)
     tw2 = send(("aa",), size, lambda t: tw2_ref.at[t["aa"]], lambda m: t2_ref.at[m["aa"]], s2, r2)
     tw3 = send(("ba",), size, lambda t: tw3_ref.at[t["ba"]], lambda m: t3_ref.at[m["ba"]], s3, r3)
 
@@ -201,15 +181,11 @@
         both = dot3(split(x_ref[i].reshape(h2 * h3, c)), (wh_ref[...], wl_ref[...]))
         sig = jax.nn.sigmoid(both[:, :c]).reshape(h2, h3, c)
         sig_ref[i] = sig
-        g_buf[i] = cot_ref[i] * sig
-        s_buf[i] = tw1_ref[i] * both[:, c:].reshape(h2, h3, c)
+        grad_ref[i] = cot_ref[i] * sig
+        first_ref[i] = tw1_ref[i] * both[:, c:].reshape(h2, h3, c)
 
     loop(h1, work)
-    first = send(("aa",), size, lambda t: s_buf.at[:, block(t["aa"], q)],
-                 lambda m: f1_ref.at[block(m["aa"], h1)], sa, ra)
-    third = send(("col",), size, lambda t: g_buf.at[:, block(t["col"], r)],
-                 lambda m: g3_ref.at[:, :, block(m["col"], h3), :], sc, rc)
-    finish(tw2, tw3, first, third)
+    finish(tw2, tw3)
 
 
 def greet(size):
@@ -228,111 +204,182 @@
     pl.semaphore_wait(sem, count)
 
 
-def kernel_two(size, f1_ref, g3_ref, m1h, m1l, m3h, m3l, tw2_ref, f2_ref, g2_ref,
-               s_buf, g_buf, sa, ra, sb, rb):
-    n1, q, h3, c = f1_ref.shape
-    h1, r, n3, _ = g3_ref.shape
-    p = f2_ref.shape[0]
-    h2 = r * size["col"]
+def part(k):
+    return slice(k * SUB, (k + 1) * SUB)
+
+
+def pairs(count):
+    return 2 if count % 2 == 0 else 1
+
+
+def kernel_main(size, first_ref, grad_ref, m1h, m1l, m1th, m1tl, m2h, m2l, m3h, m3l, m3th, m3tl,
+                tw2_ref, tw3_ref,
+                f1, f2, f3, g3, g2, g1, mixed_ref, g0_ref, raw1_ref, raw2_ref, raw3_ref,
+                wf1, wg1, wf2, wg2, wf3, wg3, s_l1, s_l2, g_l2, g_l3, acc1, acc2, acc3, load_sem,
+                sa1, ra1, sa2, ra2, sa3, ra3, sa4, ra4, sb4, rb4, sb3, rb3, sb2, rb2, sb1, rb1):
+    n1, q, h3, c = f1.shape
+    p, n2, _, _ = f2.shape
+    h1, r, n3, _ = f3.shape
+    na, nb, nc = size["aa"], size["ba"], size["col"]
+    steps = range(h3 // SUB)
+    half = wf3.shape[0]
     greet(size)
 
-    def mix_first(j):
-        out = dot3((m1h[...], m1l[...]), split(gather_first(f1_ref, j)))
-        scatter_first(s_buf, j, out * gather_first(tw2_ref, j))
-
-    loop(q, mix_first)
-    fwd = send(("aa", "ba"), size, lambda t: s_buf.at[block(t["aa"] * size["ba"] + t["ba"], p)],
-               lambda m: f2_ref.at[:, block(m["ba"] * size["aa"] + m["aa"], q)], sa, ra)
-
-    def back_third(i):
-        scatter_third(g_buf, i, dot3((m3h[...], m3l[...]), split(gather_third(g3_ref, i))))
-
-    loop(h1, back_third)
-    bwd = send(("ba", "col"), size,
-               lambda t: g_buf.at[block(t["ba"], p), :, block(t["col"], h3), :],
-               lambda m: g2_ref.at[:, block(m["ba"] * size["col"] + m["col"], r)], sb, rb)
-    finish(fwd, bwd)
-
-
-def kernel_three(size, f2_ref, g2_ref, m2h, m2l, m2th, m2tl, tw3_ref, f3_ref, g1_ref, raw_ref,
-                 s_buf, g_buf, acc, sa, ra, sb, rb):
-    p, n2, h3, c = f2_ref.shape
-    r = f3_ref.shape[1]
-    q = g1_ref.shape[1]
-    h2 = r * size["col"]
-    greet(size)
-
-    def mix_second(i):
-        out = dot3((m2h[...], m2l[...]), split(gather_second(f2_ref, i)))
-        scatter_second(s_buf, i, out * gather_second(tw3_ref, i))
-
-    loop(p, mix_second)
-    fwd = send(("ba", "col"), size,
-               lambda t: s_buf.at[:, block(t["ba"] * size["col"] + t["col"], r)],
-               lambda m: f3_ref.at[block(m["ba"], p), :, block(m["col"], h3), :], sb, rb)
-
-    def back_second(i):
-        grad = gather_second(tw3_ref, i) * gather_second(g2_ref, i)
-        scatter_second(g_buf, i, dot3((m2th[...], m2tl[...]), split(grad)))
-
-    loop(p, back_second)
-    bwd = send(("aa", "ba"), size,
-               lambda t: g_buf.at[:, block(t["ba"] * size["aa"] + t["aa"], q)],
-               lambda m: g1_ref.at[block(m["aa"] * size["ba"] + m["ba"], p)], sa, ra)
-
-    acc[...] = jnp.zeros_like(acc)
-
-    def raw(i):
-        ahead = split(gather_second(f2_ref, i))
-        grad = split(gather_second(tw3_ref, i) * gather_second(g2_ref, i))
+    def load(source, target):
+        copy = pltpu.make_async_copy(source, target, load_sem)
+        copy.start()
+        copy.wait()
+
+    def take_l1(ref, j, k):
+        return lanes([ref[:, j + t, k, :].reshape(n1 * SUB, c) for t in range(pairs(q))])
+
+    def put_l1(ref, j, k, value):
+        for t in range(pairs(q)):
+            ref[:, j + t, k, :] = value[:, t * c:(t + 1) * c].reshape(n1, SUB, c)
+
+    def take_l2(ref, i, k):
+        return lanes([ref[i + t, :, k, :].reshape(n2 * SUB, c) for t in range(pairs(p))])
+
+    def put_l2(ref, i, k, value):
+        for t in range(pairs(p)):
+            ref[i + t, :, k, :] = value[:, t * c:(t + 1) * c].reshape(n2, SUB, c)
+
+    t1 = [
+        send(("aa",), size, lambda t: first_ref.at[:, block(t["aa"], q), part(k), :],
+             lambda m: f1.at[block(m["aa"], h1), :, part(k), :], sa1.at[k], ra1.at[k])
+        for k in steps
+    ]
+    b4 = send(("col",), size, lambda t: grad_ref.at[:, block(t["col"], r)],
+              lambda m: g3.at[:, :, block(m["col"], h3), :], sb4, rb4)
+
+    t2 = []
+    for k in steps:
+        finish(t1[k])
+        load(f1.at[:, :, part(k), :], wf1)
+
+        def mix_first(i):
+            j = i * pairs(q)
+            out = dot3((m1h[...], m1l[...]), split(take_l1(wf1, j, part(0))))
+            put_l1(s_l1, j, part(k), out * take_l1(tw2_ref, j, part(k)))
+
+        loop(q // pairs(q), mix_first)
+        t2.append(send(("aa", "ba"), size,
+                       lambda t: s_l1.at[block(t["aa"] * nb + t["ba"], p), :, part(k), :],
+                       lambda m: f2.at[:, block(m["ba"] * na + m["aa"], q), part(k), :],
+                       sa2.at[k], ra2.at[k]))
+
+    finish(b4)
+    for h in range(h1 // half):
+        load(g3.at[h * half:(h + 1) * half], wg3)
+
+        def back_third(i):
+            out = dot3((m3th[...], m3tl[...]), split(gather_third(wg3, i)))
+            scatter_third(g_l3, h * half + i, out)
+
+        loop(half, back_third)
+    b3 = [
+        send(("ba", "col"), size,
+             lambda t: g_l3.at[block(t["ba"], p), :, pl.ds(pl.multiple_of(t["col"] * h3 + k * SUB, SUB), SUB), :],
+             lambda m: g2.at[:, block(m["ba"] * nc + m["col"], r), part(k), :],
+             sb3.at[k], rb3.at[k])
+        for k in steps
+    ]
+
+    t3 = []
+    for k in steps:
+        finish(t2[k])
+        load(f2.at[:, :, part(k), :], wf2.at[:, :, part(k), :])
+
+        def mix_second(i):
+            j = i * pairs(p)
+            out = dot3((m2h[...], m2l[...]), split(take_l2(wf2, j, part(k))))
+            put_l2(s_l2, j, part(k), out * take_l2(tw3_ref, j, part(k)))
+
+        loop(p // pairs(p), mix_second)
+        t3.append(send(("ba", "col"), size,
+                       lambda t: s_l2.at[:, block(t["ba"] * nc + t["col"], r), part(k), :],
+                       lambda m: f3.at[block(m["ba"], p), :, pl.ds(pl.multiple_of(m["col"] * h3 + k * SUB, SUB), SUB), :],
+                       sa3.at[k], ra3.at[k]))
+
+    b2 = []
+    for k in steps:
+        finish(b3[k])
+        load(g2.at[:, :, part(k), :], wg2.at[:, :, part(k), :])
+
+        def back_second(i):
+            j = i * pairs(p)
+            grad = take_l2(tw3_ref, j, part(k)) * take_l2(wg2, j, part(k))
+            put_l2(wg2, j, part(k), grad)
+            put_l2(g_l2, j, part(k), dot3((m2h[...], m2l[...]), split(grad), TN))
+
+        loop(p // pairs(p), back_second)
+        b2.append(send(("aa", "ba"), size,
+                       lambda t: g_l2.at[:, block(t["ba"] * na + t["aa"], q), part(k), :],
+                       lambda m: g1.at[block(m["aa"] * nb + m["ba"], p), :, part(k), :],
+                       sb2.at[k], rb2.at[k]))
+
+    acc2[...] = jnp.zeros_like(acc2)
+
+    def raw_second(i):
+        ahead = split(gather_second(wf2, i))
+        grad = split(gather_second(wg2, i))
         for s in range(0, n2 * SUB, 128):
-            acc[s:s + 128, :] += dot3((grad[0][s:s + 128], grad[1][s:s + 128]), ahead, NT)
-
-    loop(p, raw)
-    raw_ref[...] = fold_inner(acc[...], n2)
-    finish(fwd, bwd)
-
-
-def kernel_four(size, f3_ref, g1_ref, f1_ref, g3_ref, m3h, m3l, m1h, m1l, tw2_ref,
-                mixed_ref, g0_ref, raw1_ref, raw3_ref, s_buf, g_buf, acc1, acc3,
-                sa, ra, sb, rb):
-    h1, r, n3, c = f3_ref.shape
-    n1, q, h3, _ = f1_ref.shape
-    barrier([(("aa",), None), (("col",), None)], size)
-
-    def mix_third(i):
-        scatter_third(s_buf, i, dot3((m3h[...], m3l[...]), split(gather_third(f3_ref, i))))
-
-    loop(h1, mix_third)
-    fwd = send(("col",), size, lambda t: s_buf.at[:, :, block(t["col"], h3), :],
-               lambda m: mixed_ref.at[:, block(m["col"], r)], sb, rb)
-
-    def back_first(j):
-        grad = gather_first(tw2_ref, j) * gather_first(g1_ref, j)
-        scatter_first(g_buf, j, dot3((m1h[...], m1l[...]), split(grad)))
-
-    loop(q, back_first)
-    bwd = send(("aa",), size, lambda t: g_buf.at[block(t["aa"], h1)],
-               lambda m: g0_ref.at[:, block(m["aa"], q)], sa, ra)
+            acc2[s:s + 128, :] += dot3((grad[0][s:s + 128], grad[1][s:s + 128]), ahead, NT)
+
+    loop(p, raw_second)
+    raw2_ref[...] = fold_inner(acc2[...], n2)
+
+    finish(*t3)
+    for h in range(h1 // half):
+        load(f3.at[h * half:(h + 1) * half], wf3)
+
+        def mix_third(i):
+            out = dot3((m3h[...], m3l[...]), split(gather_third(wf3, i)))
+            scatter_third(g_l3, h * half + i, out)
+
+        loop(half, mix_third)
+    t4 = send(("col",), size, lambda t: g_l3.at[:, :, block(t["col"], h3), :],
+              lambda m: mixed_ref.at[:, block(m["col"], r)], sa4, ra4)
+
+    acc3[...] = jnp.zeros_like(acc3)
+    for h in range(h1 // half):
+        load(f3.at[h * half:(h + 1) * half], wf3)
+        load(g3.at[h * half:(h + 1) * half], wg3)
+
+        def raw_third(i):
+            acc3[...] += dot3(split(gather_third(wg3, i)), split(gather_third(wf3, i)), NT)
+
+        loop(half, raw_third)
+    raw3_ref[...] = fold_outer(acc3[...], n3)
 
     acc1[...] = jnp.zeros_like(acc1)
-    acc3[...] = jnp.zeros_like(acc3)
-
-    def raw_first(j):
-        ahead = split(gather_first(f1_ref, j))
-        grad = split(gather_first(tw2_ref, j) * gather_first(g1_ref, j))
-        for s in range(0, n1 * SUB, 128):
-            acc1[s:s + 128, :] += dot3((grad[0][s:s + 128], grad[1][s:s + 128]), ahead, NT)
-
-    loop(q, raw_first)
-
-    def raw_third(i):
-        acc3[...] += dot3(split(gather_third(g3_ref, i)), split(gather_third(f3_ref, i)), NT)
-
-    loop(h1, raw_third)
+    b1 = []
+    for k in steps:
+        finish(b2[k])
+        load(g1.at[:, :, part(k), :], wg1)
+
+        def back_first(i):
+            j = i * pairs(q)
+            grad = take_l1(tw2_ref, j, part(k)) * take_l1(wg1, j, part(0))
+            put_l1(wg1, j, part(0), grad)
+            put_l1(s_l1, j, part(k), dot3((m1th[...], m1tl[...]), split(grad)))
+
+        loop(q // pairs(q), back_first)
+        b1.append(send(("aa",), size, lambda t: s_l1.at[block(t["aa"], h1), :, part(k), :],
+                       lambda m: g0_ref.at[:, block(m["aa"], q), part(k), :],
+                       sb1.at[k], rb1.at[k]))
+        load(f1.at[:, :, part(k), :], wf1)
+
+        def raw_first(i):
+            j = i * pairs(q)
+            ahead = split(take_l1(wf1, j, part(0)))
+            grad = split(take_l1(wg1, j, part(0)))
+            for s in range(0, n1 * SUB, 128):
+                acc1[s:s + 128, :] += dot3((grad[0][s:s + 128], grad[1][s:s + 128]), ahead, NT)
+
+        loop(q // pairs(q), raw_first)
     raw1_ref[...] = fold_inner(acc1[...], n1)
-    raw3_ref[...] = fold_outer(acc3[...], n3)
-    finish(fwd, bwd)
+    finish(t4, *b1)
 
 
 def kernel_five(x_ref, cot_ref, sig_ref, mixed_ref, g0_ref, tw1_ref, wh_ref, wl_ref,
@@ -372,7 +419,8 @@
 
 
 def sems(*counts):
-    return [pltpu.SemaphoreType.DMA((n,)) for n in counts for _ in range(2)]
+    shapes = [n if isinstance(n, tuple) else (n,) for n in counts]
+    return [pltpu.SemaphoreType.DMA(n) for n in shapes for _ in range(2)]
 
 
 def on_device(inputs, cotangent, w_gate, w_value, mix_first, mix_second, mix_third,
@@ -403,7 +451,6 @@
     k1 = split_weight(expand(mix_first, True))
     k1t = split_weight(expand(mix_first.T, True))
     k2 = split_weight(expand(mix_second, True))
-    k2t = split_weight(expand(mix_second.T, True))
     k3 = split_weight(expand(mix_third, False))
     k3t = split_weight(expand(mix_third.T, False))
     w = split_weight(jnp.concatenate([w_gate, w_value], axis=1))
@@ -411,33 +458,28 @@
     tw2s = twiddle_second.reshape(h1, na, q * h3).transpose(1, 0, 2)
     tw3s = twiddle_third.reshape(nb, p, h2 * h3)
 
-    f1, g3, sig, t2, t3 = call(
+    first, grad, sig, t2, t3 = call(
         functools.partial(kernel_one, size), 0,
-        (sds(*l1), sds(*l3), sds(*home), sds(na, h1, q * h3), sds(nb, p, h2 * h3)),
-        (any_, any_, vm, any_, any_), [vm] * 5 + [any_] * 2,
-        [VMEM(home, F32), VMEM(home, F32)] + sems(na, nc, na, nb),
+        (sds(*home), sds(*home), sds(*home), sds(na, h1, q * h3), sds(nb, p, h2 * h3)),
+        (vm, vm, vm, any_, any_), [vm] * 5 + [any_] * 2, sems(na, nb),
         inputs, cotangent, *w, tw1, tw2s, tw3s)
     tw2 = wide(t2.reshape(n1, q, h3))
     tw3 = wide(t3.reshape(nb, p, h2, h3).transpose(1, 0, 2, 3).reshape(p, n2, h3))
 
-    f2, g2 = call(
-        functools.partial(kernel_two, size), 1, (sds(*l2), sds(*l2)), (any_, any_), [vm] * 7,
-        [VMEM(l1, F32), VMEM(l3, F32)] + sems(na * nb, nb * nc),
-        f1, g3, *k1, *k3t, tw2)
-
-    f3, g1, raw2 = call(
-        functools.partial(kernel_three, size), 2, (sds(*l3), sds(*l1), sds(n2, n2)),
-        (any_, any_, vm), [vm] * 7,
-        [VMEM(l2, F32), VMEM(l2, F32), VMEM((n2 * SUB, n2 * SUB), F32)] + sems(na * nb, nb * nc),
-        f2, g2, *k2, *k2t, tw3)
-
-    mixed, g0, raw1, raw3 = call(
-        functools.partial(kernel_four, size), 3,
-        (sds(*home), sds(*home), sds(n1, n1), sds(n3, n3)),
-        (any_, any_, vm, vm), [vm] * 9,
-        [VMEM(l3, F32), VMEM(l1, F32), VMEM((n1 * SUB, n1 * SUB), F32),
-         VMEM((n3 * SUB, n3 * SUB), F32)] + sems(na, nc),
-        f3, g1, f1, g3, *k3, *k1t, tw2)
+    nk = h3 // SUB
+    half = max(h1 // 2, 1)
+    *_, mixed, g0, raw1, raw2, raw3 = call(
+        functools.partial(kernel_main, size), 1,
+        (sds(*l1), sds(*l2), sds(*l3), sds(*l3), sds(*l2), sds(*l1), sds(*home), sds(*home),
+         sds(n1, n1), sds(n2, n2), sds(n3, n3)),
+        (any_,) * 8 + (vm,) * 3,
+        [any_] * 2 + [vm] * 12,
+        [VMEM((n1, q, SUB, c), F32)] * 2 + [VMEM(l2, F32)] * 2 + [VMEM((half, r, n3, c), F32)] * 2
+        + [VMEM(l1, F32), VMEM(l2, F32), VMEM(l2, F32), VMEM(l3, F32)]
+        + [VMEM((n * SUB, n * SUB), F32) for n in (n1, n2, n3)]
+        + [pltpu.SemaphoreType.DMA(())]
+        + sems((nk, na), (nk, na * nb), (nk, nb * nc), nc, nc, (nk, nb * nc), (nk, na * nb), (nk, na)),
+        first, grad, *k1, *k1t, *k2, *k3, *k3t, tw2, tw3)
 
     row = pl.BlockSpec((1, h2, h3, c), lambda i: (i, 0, 0, 0))
     whole = lambda *s: pl.BlockSpec(s, lambda i: (0,) * len(s))
@@ -457,7 +499,7 @@
     parts = jnp.pad(flat, (0, padded - flat.shape[0])).reshape(n, -1, 128)
     factor = float(n1 * n2 * n3) ** (-0.5)
     summed = call(
-        functools.partial(kernel_sum, size, factor), 4, sds(*parts.shape), vm, [vm],
+        functools.partial(kernel_sum, size, factor), 2, sds(*parts.shape), vm, [vm],
         [VMEM(parts.shape, F32), VMEM(parts.shape[1:], F32)] + sems(n, n), parts).reshape(-1)
     at = 0
     order = ((c, c), (c, c), (n2, n2), (n1, n1), (n3, n3))

time: 609 us -> 538 us (0.88)
  Pallas kernels: 564 us -> 495 us
    pallas_call x5 -> x3, Pallas kernels: 546 us -> 476 us  [call(): pl.pallas_call(body, out_shape=outs, in_specs=in_specs, out_specs=out_spe...]
    dot_general x6 -> x5, matrix products: 15.7 us -> 11 us  [expand(): jnp.dot(jnp.dot(pick, m, precision=highest), pick.T, precision=highest)]
where the time goes in v2:
time: 538 us; the launch traced here: 536 us
  Pallas kernels  495 us (92%)
  local copies, waits for them, and re-layouts  22.4 us (4%)
  matrix products  17.2 us (3%)
    pallas_call x3, Pallas kernels, call(): pl.pallas_call(body, out_shape=outs, in_specs=in_specs, out_specs=out_spe...  476 us
    pallas_call x1, Pallas kernels, on_device(): pl.pallas_call(kernel_five, grid=(h1,), out_shape=(sds(*home), sds(*home)...  18.4 us
    dot_general x5, matrix products, expand(): jnp.dot(jnp.dot(pick, m, precision=highest), pick.T, precision=highest)  11 us

profile of v2, /device:TPU:0, one launch (start us, length us, event | category | flops | bytes accessed | tf_op | source)
XLA Modules:
  0.0 536.1 jit_solution(7132322328306820494)
XLA Ops:
  0.6 0.0 copy-start
  0.6 0.0 copy-start.2
  0.8 1.1 fusion.18
  1.8 1.1 fusion.17
  2.9 1.3 fusion.12
  4.2 1.3 fusion.13
  5.4 0.8 constant_dynamic-update-slice_fusion.1
  6.3 0.8 constant_dynamic-update-slice_fusion
  7.1 0.7 fusion.16
  7.8 1.2 fusion.7
  9.0 1.2 fusion.6
  10.2 1.0 copy.24
  11.2 1.0 copy.25
  12.3 0.1 reshape.68
  12.4 0.6 copy.33
  13.0 0.0 copy-done.2
  13.0 0.1 copy.27
  13.2 0.8 reshape.69.tw3_ref
  13.9 0.0 copy-done
  13.9 1.6 fusion.5
  15.5 2.0 fusion.2
  17.5 2.0 fusion.3
  19.5 4.7 fusion
  24.1 2.6 broadcast_in_dim.34.tw1_ref
  26.7 20.2 %shard_map.153 = (f32[16,32,16,128]{3,2,1,0:T(8,128)}, f32[16,32,16,128]{3,2,1,0:T(8,128)}, f32[16,32,16,128]{3,2,1,0:T(8,128)}, f32[4,16,128]{2,1,0:T(8,128)}, f32[4,4,512]{2,1,0:T(4,128)}) custom-call(f32[16,32,16,128]{3,2,1,0:T(8,128)} %x_ref.3, f32[16,32,16,128]{3,2,1,0:T(8,128)} %cot_ref.3, bf16[128,256]{1,0:T(8,128)(2,1)} %get-tuple-element.49.wh_ref, ...), custom_call_target="tpu_custom_call" | custom-call | tf_op jit(solution)/shard_map/pallas_call | solution.py:439
  46.9 0.9 broadcast_in_dim.38
  47.8 0.9 reshape.70
  48.7 2.6 broadcast_in_dim.41.tw3_ref
  51.4 2.6 broadcast_in_dim.39.tw2_ref
  54.0 429.4 %shard_map.154 = (f32[64,8,16,128]{3,2,1,0:T(8,128)}, f32[4,128,16,128]{3,2,1,0:T(8,128)}, f32[16,16,32,128]{3,2,1,0:T(8,128)}, f32[16,16,32,128]{3,2,1,0:T(8,12...) custom-call(f32[16,32,16,128]{3,2,1,0:T(8,128)} %get-tuple-element.2, ...), custom_call_target="tpu_custom_call" | custom-call | tf_op jit(solution)/shard_map/pallas_call | solution.py:439
  483.4 0.0 copy-start.5
  483.4 0.0 copy-start.4
  483.4 0.0 copy-start.3
  483.4 0.0 copy-start.1
  483.5 18.4 %shard_map.155 = (f32[16,32,16,128]{3,2,1,0:T(8,128)}, f32[16,32,16,128]{3,2,1,0:T(8,128)}, f32[128,128]{1,0:T(8,128)}, f32[128,128]{1,0:T(8,128)}) custom-call(f32[16,32,16,128]{3,2,1,0:T(8,128)} %x_ref.3, f32[16,32,16,128]{3,2,1,0:T(8,128)} %cot_ref.3, f32[16,32,16,128]{3,2,1,0:T(8,128)} %get-tuple-element.21.sig_ref, ...), custom_call_target="tpu_custom_call" | custom-call | tf_op jit(solution)/shard_map/pallas_call | solution.py:486
  501.8 0.0 copy-done.5
  501.9 0.1 reshape.75
  501.9 0.1 reshape.74
  502.0 0.8 bitcast_dynamic-update-slice_fusion.2
  502.9 0.8 bitcast_dynamic-update-slice_fusion.1
  503.7 0.0 copy-done.3
  503.7 0.7 pad.4
  504.5 26.8 %shard_map.156 = f32[32,16,128]{2,1,0:T(8,128)} custom-call(f32[32,16,128]{2,1,0:T(8,128)} %bitcast.26), custom_call_target="tpu_custom_call" | custom-call | tf_op jit(solution)/shard_map/pallas_call | solution.py:439
  531.3 0.7 slice.24
  532.0 0.7 reshape.79
  532.7 1.6 fusion.57
  534.3 1.2 slice.26
  535.5 0.6 slice.28
  (15 shorter events, 0.1 us)
Async XLA Ops:
  0.6 13.3 %copy-start = (f32[128,128]{1,0:T(8,128)S(1)}, f32[128,128]{1,0:T(8,128)}, u32[]{:S(2)}) copy-start(f32[128,128]{1,0:T(8,128)} %param.15) | copy-start | bytes 196612
  0.6 12.4 %copy-start.2 = (f32[16,32,16]{1,2,0:T(8,128)S(1)}, f32[16,32,16]{1,2,0:T(8,128)}, u32[]{:S(2)}) copy-start(f32[16,32,16]{1,2,0:T(8,128)} %param.19) | copy-start | bytes 98308
  483.4 18.4 %copy-start.5 = (f32[32,32]{1,0:T(8,128)S(1)}, f32[32,32]{1,0:T(8,128)}, u32[]{:S(2)}) copy-start(f32[32,32]{1,0:T(8,128)} %get-tuple-element.34) | copy-start | bytes 12292
  483.4 18.5 %copy-start.4 = (f32[64,64]{1,0:T(8,128)S(1)}, f32[64,64]{1,0:T(8,128)}, u32[]{:S(2)}) copy-start(f32[64,64]{1,0:T(8,128)} %get-tuple-element.33) | copy-start | bytes 49156
  483.4 20.3 %copy-start.3 = (f32[128,128]{1,0:T(8,128)S(1)}, f32[128,128]{1,0:T(8,128)}, u32[]{:S(2)}) copy-start(f32[128,128]{1,0:T(8,128)} %get-tuple-element.32) | copy-start | bytes 196612
  483.4 52.7 %copy-start.1 = (f32[128,128]{1,0:T(8,128)S(1)}, f32[128,128]{1,0:T(8,128)}, u32[]{:S(2)}) copy-start(f32[128,128]{1,0:T(8,128)} %param.15) | copy-start | bytes 196612
